TPU v7x, 128 devices: a whole 4x4x4 slice. The times are simulated.
128 devices in a mesh: seq: 8 (over z, core), exp: 16 (over y, x).
Axes of the slice: x: 4, y: 4, z: 4, core: 2. Of those that a mesh axis runs over, the one named last changes fastest.
Arguments:
- tokens: bfloat16 [16384, 2048], P(('seq', 'exp')), may hold values from -6 to 6
- norm_in: float32 [2048], replicated, may hold values from 0.1 to 1.9
- w_query: bfloat16 [2048, 2048], P(None, 'exp'), may hold values from -0.125 to 0.125
- w_key: bfloat16 [2048, 2048], P(None, 'exp'), may hold values from -0.125 to 0.125
- w_value: bfloat16 [2048, 4096], P(None, 'exp'), may hold values from -0.125 to 0.125
- w_outgate: bfloat16 [2048, 4096], P(None, 'exp'), may hold values from -0.125 to 0.125
- log_decay: float32 [32, 16384], P('exp', 'seq'), may hold values from -1 to 0, as said below
- write_rate: float32 [32, 16384], P('exp', 'seq'), may hold values from 0.005 to 0.95
- head_gain: float32 [128], replicated, may hold values from 0.1 to 1.9
- w_output: bfloat16 [4096, 2048], P('exp'), may hold values from -0.09375 to 0.09375
- norm_post: float32 [2048], replicated, may hold values from 0.1 to 1.9
- route_ids: int32 [16384, 10], P('seq'), may hold values from 0 to 31, all different within a row; in each aligned block of 128 rows (0 to 127, 128 to 255, ...) at most 80 rows name the same one
- route_weights: float32 [16384, 10], P('seq'), may hold values from 0.1 to 0.5
- w_gate: bfloat16 [32, 2048, 512], P('exp'), may hold values from -0.125 to 0.125
- w_up: bfloat16 [32, 2048, 512], P('exp'), may hold values from -0.125 to 0.125
- w_down: bfloat16 [32, 512, 2048], P('exp'), may hold values from -0.25 to 0.25
- w_shared_gate: bfloat16 [2048, 512], replicated, may hold values from -0.125 to 0.125
- w_shared_up: bfloat16 [2048, 512], replicated, may hold values from -0.125 to 0.125
- w_shared_down: bfloat16 [512, 2048], replicated, may hold values from -0.25 to 0.25
- w_shared_switch: bfloat16 [2048], replicated, may hold values from -0.125 to 0.125
Outputs:
- layer_out: bfloat16 [16384, 2048], P(('seq', 'exp'))
Inputs may be any that keep to these rules, and one draw needn't show every extreme that they name: `route_ids`: each row names 10 different experts. In each aligned block of 128 rows (the tokens of one device) no expert is named by more than 80 rows. `log_decay`: never positive.
All inputs are finite; a program needn't handle non-finite values.
Results may differ from a plain program's by a relative error of at most 0.023.
Values may be sent and summed in bfloat16 or wider, within the bound.
No kernel may reach another device: no remote copies, remote signals or barrier semaphores. Data moves between devices by JAX's collectives and lax.ppermute only.
A program may use at most 192 MiB of HBM per device.

v0:
```python
import jax
import jax.numpy as jnp
from jax import lax
from jax.sharding import PartitionSpec as P

DK = 128
DV = 128


largest_value = lax.Precision.HIGHEST


def shifted(value, axis, by):
    peers = lax.axis_size(axis)
    pairs = [(i, i + by) for i in range(peers) if 0 <= i + by < peers]
    return lax.ppermute(value, axis, pairs)


def row_norm(values, gain_vec, epsilon):
    return (
        values * lax.rsqrt(jnp.mean(values * values, axis=-1, keepdims=True) + epsilon) * gain_vec
    )


def unit_rows(values):
    return values * lax.rsqrt(jnp.sum(values * values, axis=-1, keepdims=True) + 1e-06)


def block_terms(queries, key_rows, values, log_rates, strengths):
    length = queries.shape[-2]
    positions = jnp.arange(length, dtype=jnp.int32)
    causal = positions[:, None] >= positions[None, :]
    strict = positions[:, None] > positions[None, :]
    cumulative = jnp.cumsum(log_rates, axis=-1)
    spread_log = cumulative[..., :, None] - cumulative[..., None, :]
    ratios = jnp.where(causal, jnp.exp(jnp.where(causal, spread_log, 0.0)), 0.0)
    key_key = jnp.einsum("...td,...sd->...ts", key_rows, key_rows, precision=largest_value)
    query_key = jnp.einsum("...td,...sd->...ts", queries, key_rows, precision=largest_value)
    lower_part = jnp.where(strict, ratios * key_key * strengths[..., None, :], 0.0)
    identity = jnp.eye(length, dtype=jnp.float32)
    decays = jnp.exp(cumulative)
    stacked = jnp.concatenate([values, decays[..., None] * key_rows], axis=-1)
    solved = jax.scipy.linalg.solve_triangular(
        identity + lower_part, stacked, lower=True, unit_diagonal=True
    )
    value_width = values.shape[-1]
    updates = solved[..., :value_width]
    weights = solved[..., value_width:]
    mixing = ratios * query_key * strengths[..., None, :]
    local_out = jnp.einsum("...ts,...sv->...tv", mixing, updates, precision=largest_value)
    query_eff = decays[..., None] * queries - jnp.einsum(
        "...ts,...sk->...tk", mixing, weights, precision=largest_value
    )
    to_end = jnp.exp(cumulative[..., -1:] - cumulative) * strengths
    key_tail = key_rows * to_end[..., None]
    key_width = key_rows.shape[-1]
    transit = decays[..., -1, None, None] * jnp.eye(key_width, dtype=jnp.float32) - jnp.einsum(
        "...tk,...tl->...kl", key_tail, weights, precision=largest_value
    )
    inject = jnp.einsum("...tk,...tv->...kv", key_tail, updates, precision=largest_value)
    return (local_out, query_eff, transit, inject)


def run_blocks(current_state, local_out, query_eff, transit, inject):

    def advance(running_total, per_block):
        output_part, effective_part, transfer_part, addition_part = per_block
        final_result = output_part + jnp.einsum(
            "rjw,rwe->rje", effective_part, running_total, precision=largest_value
        )
        running_total = (
            jnp.einsum("eca,eaj->ecj", transfer_part, running_total, precision=largest_value)
            + addition_part
        )
        return (running_total, final_result)

    per_block = (
        jnp.moveaxis(local_out, 1, 0),
        jnp.moveaxis(query_eff, 1, 0),
        jnp.moveaxis(transit, 1, 0),
        jnp.moveaxis(inject, 1, 0),
    )
    final_state, outputs = lax.scan(advance, current_state, per_block)
    return jnp.moveaxis(outputs, 0, 1)


def compose_maps(earlier_map, later_map):
    move_first, first_addition = earlier_map
    second_transfer, second_addition = later_map
    moved = jnp.einsum("hkl,hlm->hkm", second_transfer, move_first, precision=largest_value)
    addition_result = (
        jnp.einsum("eca,eaj->ecj", second_transfer, first_addition, precision=largest_value)
        + second_addition
    )
    return (moved, addition_result)


def slot_table(flat_rows, experts, capacity):
    flat_ids = flat_rows.reshape(-1)
    onehot = (flat_ids[:, None] == jnp.arange(experts, dtype=jnp.int32)[None, :]).astype(jnp.int32)
    slot_rank = jnp.sum(
        (jnp.cumsum(onehot, axis=0, dtype=jnp.int32) - onehot) * onehot, axis=1, dtype=jnp.int32
    )
    targets = flat_ids * capacity + slot_rank
    entries = jnp.arange(flat_ids.shape[0], dtype=jnp.int32)
    inverse = jnp.full((experts * capacity,), -1, jnp.int32).at[targets].set(entries)
    return (inverse, targets)


def expert_apply(received, w_gate, w_up, w_down):
    gate_part = jnp.einsum("sjcd,jdf->sjcf", received, w_gate, preferred_element_type=jnp.float32)
    up_part = jnp.einsum("sjcd,jdf->sjcf", received, w_up, preferred_element_type=jnp.float32)
    hidden = (jax.nn.silu(gate_part) * up_part).astype(jnp.bfloat16)
    return jnp.einsum("sjcf,jfd->sjcd", hidden, w_down, preferred_element_type=jnp.float32).astype(
        jnp.bfloat16
    )


def local(
    tokens,
    norm_in,
    w_query,
    w_key,
    w_value,
    w_outgate,
    log_decay,
    write_rate,
    head_gain,
    w_output,
    norm_post,
    route_ids,
    route_weights,
    w_gate,
    w_up,
    w_down,
    w_shared_gate,
    w_shared_up,
    w_shared_down,
    w_shared_switch,
):
    tok_dev = tokens.shape[0]
    model_width = tokens.shape[1]
    owners = lax.axis_size("exp")
    tok_seq = tok_dev * owners
    position = lax.axis_index("exp")
    residual_in = tokens.astype(jnp.float32)
    normed = row_norm(residual_in, norm_in, 1e-06).astype(jnp.bfloat16)
    w_all = jnp.concatenate([w_query, w_key, w_value, w_outgate], axis=1)
    projected = jnp.dot(
        lax.all_gather(normed, "exp", axis=0, tiled=True), w_all, preferred_element_type=jnp.float32
    )
    query_cols = w_query.shape[1]
    key_cols = w_key.shape[1]
    value_cols = w_value.shape[1]
    key_heads = query_cols // DK
    value_heads = value_cols // DV
    group_size = value_heads // key_heads
    value_start = query_cols + key_cols
    gate_start = value_start + value_cols
    query_raw = projected[:, :query_cols].reshape(tok_seq, key_heads, DK)
    key_raw = projected[:, query_cols:value_start].reshape(tok_seq, key_heads, DK)
    queries = jnp.transpose(jnp.repeat(query_raw, group_size, axis=1), (1, 0, 2))
    key_rows = jnp.transpose(jnp.repeat(unit_rows(key_raw), group_size, axis=1), (1, 0, 2))
    values = jnp.transpose(
        projected[:, value_start:gate_start].reshape(tok_seq, value_heads, DV), (1, 0, 2)
    )
    gate_proj = projected[:, gate_start:].reshape(tok_seq, value_heads, DV)
    length = min(128, tok_seq)
    blocks = tok_seq // length
    local_out, query_eff, transit, inject = block_terms(
        queries.reshape(value_heads, blocks, length, DK),
        key_rows.reshape(value_heads, blocks, length, DK),
        values.reshape(value_heads, blocks, length, DV),
        log_decay.reshape(value_heads, blocks, length),
        write_rate.reshape(value_heads, blocks, length),
    )
    identity = jnp.broadcast_to(jnp.eye(DK, dtype=jnp.float32), (value_heads, DK, DK))
    empty_state = jnp.zeros((value_heads, DK, DV), jnp.float32)

    def compose_step(running_total, per_block):
        return (compose_maps(running_total, per_block), None)

    (complete_transfer, complete_addition), _ = lax.scan(
        compose_step,
        (identity, empty_state),
        (jnp.moveaxis(transit, 1, 0), jnp.moveaxis(inject, 1, 0)),
    )

    def relay_step(counter, current_state):
        departing_rows = (
            jnp.einsum("eca,eaj->ecj", complete_transfer, current_state, precision=largest_value)
            + complete_addition
        )
        return shifted(departing_rows.astype(jnp.bfloat16), "seq", 1).astype(departing_rows.dtype)

    entering = lax.fori_loop(0, lax.axis_size("seq") - 1, relay_step, empty_state)
    attended = run_blocks(entering, local_out, query_eff, transit, inject)
    attended = jnp.transpose(attended.reshape(value_heads, tok_seq, DV), (1, 0, 2))
    gated = (
        (row_norm(attended, head_gain, 1e-06) * jax.nn.silu(gate_proj))
        .astype(jnp.bfloat16)
        .reshape(tok_seq, value_heads * DV)
    )
    mixed_out = lax.psum_scatter(
        jnp.dot(gated, w_output, preferred_element_type=jnp.float32).astype(jnp.bfloat16),
        "exp",
        scatter_dimension=0,
        tiled=True,
    ).astype(jnp.float32)
    residual = residual_in + mixed_out
    post_norm = row_norm(residual, norm_post, 1e-06).astype(jnp.bfloat16)
    switch = jax.nn.sigmoid(jnp.dot(post_norm, w_shared_switch, preferred_element_type=jnp.float32))
    inner_act = (
        jax.nn.silu(jnp.dot(post_norm, w_shared_gate, preferred_element_type=jnp.float32))
        * jnp.dot(post_norm, w_shared_up, preferred_element_type=jnp.float32)
    ).astype(jnp.bfloat16)
    shared = jnp.dot(inner_act, w_shared_down, preferred_element_type=jnp.float32) * switch[:, None]
    exp_dev = w_gate.shape[0]
    experts = exp_dev * owners
    top_count = route_ids.shape[1]
    capacity = min(tok_dev, 2 * tok_dev * top_count // experts)
    own_ids = lax.dynamic_slice_in_dim(route_ids, position * tok_dev, tok_dev, 0)
    own_weights = lax.dynamic_slice_in_dim(route_weights, position * tok_dev, tok_dev, 0)
    inverse, targets = slot_table(own_ids, experts, capacity)
    present = inverse >= 0
    token_at = jnp.maximum(inverse, 0) // top_count
    send_rows = jnp.where(present[:, None], post_norm[token_at], jnp.zeros((), jnp.bfloat16))
    send_rows = send_rows.reshape(owners, exp_dev, capacity, model_width)
    produced = expert_apply(
        lax.all_to_all(send_rows, "exp", split_axis=0, concat_axis=0, tiled=True),
        w_gate,
        w_up,
        w_down,
    )
    returned = lax.all_to_all(produced, "exp", split_axis=0, concat_axis=0, tiled=True)
    picked = returned.reshape(experts * capacity, model_width)[targets].reshape(
        tok_dev, top_count, model_width
    )
    routed = jnp.sum(own_weights[:, :, None] * picked.astype(jnp.float32), axis=1)
    return (residual + shared + routed).astype(jnp.bfloat16)


def solution(mesh):
    in_specs = (
        P(("seq", "exp"), None),
        P(),
        P(None, "exp"),
        P(None, "exp"),
        P(None, "exp"),
        P(None, "exp"),
        P("exp", "seq"),
        P("exp", "seq"),
        P(),
        P("exp", None),
        P(),
        P("seq", None),
        P("seq", None),
        P("exp", None, None),
        P("exp", None, None),
        P("exp", None, None),
        P(),
        P(),
        P(),
        P(),
    )
    out_specs = P(("seq", "exp"), None)
    return jax.shard_map(local, mesh=mesh, in_specs=in_specs, out_specs=out_specs, check_vma=False)
```

profile of v0, /device:TPU:32, one launch (start us, length us, event | category | flops | bytes accessed | tf_op | source)
XLA Modules:
  0.0 1078.2 jit_solution(2897070794162489235)
XLA Ops:
  8.0 2.0 fusion.88
  14.2 68.6 %all-gather.2.cloned.1.call-done = bf16[2048,2048]{1,0:T(8,128)(2,1)} async-done(((bf16[128,2048]{1,0:T(8,128)(2,1)}), bf16[2048,2048]{1,0:T(8,128)(2,1)}) %all-gather.2.cloned.1.call-update) | async-done | bytes 8388624 | tf_op jit(solution)/shard_map/all_gather | solution.py:150
  82.8 10.1 fusion.39
  93.1 2.2 fusion.116
  100.2 6.2 add_bitcast_fusion
  106.4 315.8 %custom-call.4 = f32[2,16,1,128,128]{3,4,2,1,0:T(8,128)} custom-call(f32[2,16,1,128,128]{4,3,2,1,0:T(8,128)} %add_bitcast_fusion), custom_call_target="InvertDiagBlocksLowerTriangular" | custom-call | tf_op jit(solution)/shard_map/jit(_solve_triangular)/vmap(vmap())/triangular_solve | solution.py:43
  422.2 3.0 copy.87
  425.2 6.6 fusion.32
  431.8 4.1 fusion.72
  436.0 4.5 bitcast_subtract_fusion.1
  443.5 39.7 %while.37 = (s32[]{:T(128)}, f32[2,128,128]{2,1,0:T(8,128)S(1)}, f32[2,128,128]{2,1,0:T(8,128)S(1)}, f32[16,2,128,128]{3,2,1,0:T(8,128)}, f32[16,2,128,128]{3,2,1,0:T(8,128)}, /*index=5*/s32[]{:T(128)}, s32[]{:T(128)}) while((s32[]{:T(128)}, f32[2,128,128]{2,1,0:T(8,128)S(1)}, f32[2,128,128]{2,1,0:T(8,128)S(1)}, ...), condition=%wide.region_4.5_spmd.clone, body=%wide.region_3.4_spmd.clone.sunk | while | flops 100728832 | bytes 1443415 | solution.py:183
  483.3 2.5 copy.119
  485.8 5.9 multiply_multiply_fusion
  491.7 3.5 fusion.69
  495.2 3.6 bitcast_subtract_fusion
  498.9 41.2 %while.38 = (s32[]{:T(128)}, f32[2,128,128]{2,1,0:T(8,128)S(1)}, f32[2,128,128]{2,1,0:T(8,128)S(1)}, f32[2,128,128]{2,1,0:T(8,128)S(1)}, s32[]{:T(128)}, /*index=5*/s32[]{:T(128)}) while((s32[]{:T(128)}, f32[2,128,128]{2,1,0:T(8,128)S(1)}, f32[2,128,128]{2,1,0:T(8,128)S(1)}, f32[2,128,128]{2,1,0:T(8,128)S(1)}, s32[]{:T(128)}, ...), condition=%wide.region_6.7_spmd.clone, body=%wide.region_5.6_spmd.clone.sunk | while | flops 50462720 | bytes 917623 | solution.py:196
  499.1 1.9 collective-permute-start
  501.1 3.7 collective-permute-done
  507.0 3.7 collective-permute-done
  512.9 3.7 collective-permute-done
  518.8 3.7 collective-permute-done
  524.7 3.7 collective-permute-done
  528.6 1.9 collective-permute-start
  530.5 3.7 collective-permute-done
  534.5 1.9 collective-permute-start
  536.4 3.7 collective-permute-done
  540.1 50.8 %while.36 = (s32[]{:T(128)}, f32[2,128,128]{2,1,0:T(8,128)S(1)}, f32[16,2,128,128]{3,2,0,1:T(8,128)}, f32[16,2,128,128]{3,2,1,0:T(8,128)}, f32[16,2,128,128]{3,2...) while((s32[]{:T(128)}, f32[2,128,128]{2,1,0:T(8,128)S(1)}, ...), condition=%wide.region_8.9_spmd, body=%wide.region_7.8_spmd.sunk | while | flops 100728832 | bytes 1312853 | solution.py:83
  590.9 2.2 fusion.56
  593.2 2.9 copy.101
  596.1 3.3 fusion.59
  601.4 6.8 convolution_convert_fusion
  609.4 9.1 reduce-window.6
  619.5 5.3 scatter_custom_fusion
  624.9 68.2 %reduce-scatter.2.cloned.1.call-done = bf16[128,2048]{1,0:T(8,128)(2,1)} async-done(((bf16[2048,2048]{1,0:T(8,128)(2,1)}), bf16[128,2048]{1,0:T(8,128)(2,1)}) %reduce-scatter.2.cloned.1.call-update) | async-done | bytes 524304 | tf_op jit(solution)/shard_map/reduce_scatter | solution.py:204
  695.7 10.8 %gather_fusion = bf16[2560,2048]{1,0:T(8,128)(2,1)} fusion(bf16[128,2048]{1,0:T(8,128)(2,1)S(1)} %multiply_convert_fusion, s32[3072]{0:T(1024)S(1)} %pad_clamp_fusion), kind=kCustom, calls=%fused_computation | custom fusion | bytes 20981760 | tf_op jit(solution)/shard_map/gather | solution.py:227
  706.4 5.7 broadcast_select_fusion
  712.1 124.1 %all_to_all.10 = bf16[16,2,80,2048]{3,2,1,0:T(8,128)(2,1)S(1)} all-to-all(bf16[16,2,80,2048]{3,2,1,0:T(8,128)(2,1)S(1)} %broadcast_select_fusion), channel_id=1, replica_groups=mesh['seq'=8,'exp'=16] {'exp'}, dimensions={0} | all-to-all | bytes 20971520 | tf_op jit(solution)/shard_map/all_to_all | solution.py:230
  836.3 7.3 fusion.24
  843.6 7.3 fusion.26
  851.0 12.5 %convert_bitcast_fusion = bf16[16,2,80,2048]{3,2,0,1:T(8,128)(2,1)} fusion(bf16[2,512,2048]{2,1,0:T(8,128)(2,1)S(1)} %copy-done.20, f32[2,16,80,512]{3,2,1,0:T(8,128)} %fusion.24, f32[2,16,80,512]{3,2,1,0:T(8,128)} %fusion.26), kind=kOutput, calls=%fused_computation.32 | convolution fusion | flops 5381816320 | bytes 25165824 | tf_op jit(solution)/shard_map/sjcf,jfd->sjcd/dot_general | solution.py:114
  863.5 10.0 copy.111
  873.5 5.2 all-to-all-start.1
  879.8 2.1 fusion.118
  881.9 148.4 %all-to-all-done.1 = bf16[16,2,80,2048]{3,2,1,0:T(8,128)(2,1)} async-done(((bf16[16,2,80,2048]{3,2,1,0:T(8,128)(2,1)}), bf16[16,2,80,2048]{3,2,1,0:T(8,128)(2,1)}, u32[]{:S(2)}, u32[]{:S(2)}) %all-to-all-start.1) | async-done | bytes 10485792 | tf_op jit(solution)/shard_map/all_to_all | solution.py:235
  1030.3 16.2 %gather_fusion.1 = bf16[1280,2048]{1,0:T(8,128)(2,1)} fusion(bf16[2560,2048]{1,0:T(8,128)(2,1)} %bitcast.37, s32[2048]{0:T(1024)S(1)} %pad_clamp_fusion.1), kind=kCustom, calls=%fused_computation.1 | custom fusion | bytes 10490880 | tf_op jit(solution)/shard_map/gather | solution.py:236
  1046.4 10.4 reshape.173
  1056.8 10.5 multiply_reduce_fusion
  1067.4 3.8 fusion.55
  (230 shorter events, 120.1 us)
Async XLA Ops:
  6.5 1060.8 %copy-start = (bf16[512,2048]{1,0:T(8,128)(2,1)S(1)}, bf16[512,2048]{1,0:T(8,128)(2,1)}, u32[]{:S(2)}) copy-start(bf16[512,2048]{1,0:T(8,128)(2,1)} %param.44) | copy-start | bytes 6291460
  6.5 3.6 copy-start.10
  6.5 3.6 copy-start.9
  6.5 76.3 %copy-start.21 = (bf16[2048,128]{1,0:T(8,128)(2,1)S(1)}, bf16[2048,128]{1,0:T(8,128)(2,1)}, u32[]{:S(2)}) copy-start(bf16[2048,128]{1,0:T(8,128)(2,1)} %param.29) | copy-start | bytes 1572868
  6.5 76.3 %all-gather.2.cloned.1.call-start = ((), (), s32[]{:S(2)}) async-start(), calls=%async_computation.3 | async-start | bytes 8912896 | tf_op jit(solution)/shard_map/all_gather | solution.py:150
  10.0 683.0 %reduce-scatter.2.cloned.1.call-start = ((), (), s32[]{:S(2)}) async-start(), calls=%async_computation.4 | async-start | bytes 8912896 | tf_op jit(solution)/shard_map/reduce_scatter | solution.py:204
  14.2 421.8 %copy-start.5 = (f32[128,128]{1,0:T(8,128)}, f32[128,128]{1,0:T(8,128)S(1)}, u32[]{:S(2)}) copy-start(f32[128,128]{1,0:T(8,128)S(1)} %get-tuple-element.221) | copy-start | bytes 196612
  98.4 1.7 copy-start.8
  98.4 1.7 copy-start.11
  98.4 1.7 copy-start.12
  98.4 1.7 copy-start.13
  431.8 4.2 copy-start.1
  431.8 4.2 copy-start.15
  442.0 1.4 copy-start.6
  485.8 5.9 copy-start.2
  491.7 3.5 copy-start.4
  491.7 3.5 copy-start.7
  499.1 5.6 collective-permute-start
  505.0 5.6 collective-permute-start
  510.9 5.6 collective-permute-start
  516.8 5.6 collective-permute-start
  522.7 5.6 collective-permute-start
  528.6 5.6 collective-permute-start
  534.5 5.6 collective-permute-start
  593.2 2.9 copy-start.17
  608.2 84.9 %copy-start.3 = (bf16[128,2048]{1,0:T(8,128)(2,1)S(1)}, bf16[128,2048]{1,0:T(8,128)(2,1)}, u32[]{:S(2)}) copy-start(bf16[128,2048]{1,0:T(8,128)(2,1)} %param.26) | copy-start | bytes 1572868
  608.2 86.2 %copy-start.14 = (f32[2048]{0:T(1024)S(1)}, f32[2048]{0:T(1024)}, u32[]{:S(2)}) copy-start(f32[2048]{0:T(1024)} %param.36) | copy-start | bytes 24580
  712.1 124.2 %copy-start.18 = (bf16[2,2048,512]{2,1,0:T(8,128)(2,1)S(1)}, bf16[2,2048,512]{2,1,0:T(8,128)(2,1)}, u32[]{:S(2)}) copy-start(bf16[2,2048,512]{2,1,0:T(8,128)(2,1)} %param.40) | copy-start | bytes 12582916
  836.3 7.3 copy-start.19
  843.6 7.3 copy-start.20
  873.5 6.0 copy-start.16
  873.5 156.8 %all-to-all-start.1 = ((bf16[16,2,80,2048]{3,2,1,0:T(8,128)(2,1)}), bf16[16,2,80,2048]{3,2,1,0:T(8,128)(2,1)}, u32[]{:S(2)}, u32[]{:S(2)}) async-start(bf16[16,2,80,2048]{3,2,1,0:T(8,128)(2,1)} %copy.111), calls=%async_computation.2 | async-start | bytes 20971520 | tf_op jit(solution)/shard_map/all_to_all | solution.py:235
Sparse Core Ops, SparseCore 0:
  10.1 72.6 all-gather.1
  608.3 84.7 reduce-scatter.1
where the time goes:
time: 1090 us; the launch traced here: 1080 us
  other arithmetic  360 us (33%)
  waiting for transfers between devices  311 us (29%)
  matrix products  175 us (16%)
  blocking collectives  124 us (11%)
  local copies, waits for them, and re-layouts  73.7 us (7%)
  starting transfers between devices  18.7 us (2%)
  between operations  14.1 us (1%)
    another operation x4, other arithmetic, block_terms(): jax.scipy.linalg.solve_triangular(identity + lower_part, stacked, lower=T...  317 us
    all_to_all x1, waiting for transfers between devices, local(): lax.all_to_all(produced, 'exp', split_axis=0, concat_axis=0, tiled=True)  148 us
    all_to_all x1, blocking collectives, local(): lax.all_to_all(send_rows, 'exp', split_axis=0, concat_axis=0, tiled=True)  124 us
    all_gather x1, waiting for transfers between devices, local(): lax.all_gather(normed, 'exp', axis=0, tiled=True)  68.6 us
    reduce_scatter x1, waiting for transfers between devices, local(): lax.psum_scatter(jnp.dot(gated, w_output, preferred_element_type=jnp.floa...  68.2 us
    dot_general x16, matrix products, advance(): jnp.einsum('rjw,rwe->rje', effective_part, running_total, precision=large...  30.4 us
    ppermute x7, waiting for transfers between devices, shifted(): return lax.ppermute(value, axis, pairs)  25.6 us
  transfers between devices with their start and end apart: 10, of which 10 were waited for; matrix products, arithmetic and copies ran while one was open for 2% of the time, Pallas kernels for 0%

commit v1 on v0

v1 whole, which is shorter than its diff:
```python
import jax
import jax.numpy as jnp
from jax import lax
from jax.experimental import pallas as pl
from jax.experimental.pallas import tpu as pltpu
from jax.sharding import PartitionSpec as P

DK = 128
DV = 128
BLOCK = 128
F32 = jnp.float32
BF16 = jnp.bfloat16
NN = (((1,), (0,)), ((), ()))
NT = (((1,), (1,)), ((), ()))
TN = (((0,), (0,)), ((), ()))


def row_norm(values, gain_vec, epsilon):
    return (
        values * lax.rsqrt(jnp.mean(values * values, axis=-1, keepdims=True) + epsilon) * gain_vec
    )


def split(x):
    hi = x.astype(BF16)
    return hi, (x - hi.astype(F32)).astype(BF16)


def mm(a, b, dims=NN):
    return lax.dot_general(a, b, dims, preferred_element_type=F32)


def dot3_narrow(a, b):
    ah, al = split(a)
    bh, bl = split(b)
    left = jnp.concatenate([ah, al], axis=1)
    right = jnp.concatenate(
        [jnp.concatenate([bh, bl], axis=1), jnp.concatenate([bh, jnp.zeros_like(bl)], axis=1)],
        axis=0,
    )
    both = mm(left, right)
    return both[:, :128] + both[:, 128:]


def dot3_wide(a, b):
    ah, al = split(a)
    bh, bl = split(b)
    return mm(jnp.concatenate([ah, al], axis=1), jnp.concatenate([bh, bh], axis=0)) + mm(ah, bl)


def delta_kernel(blocks, proj_ref, cum_ref, rate_ref, base_ref, reach_ref, total_ref, state):
    step = pl.program_id(0)
    rows = lax.broadcasted_iota(jnp.int32, (BLOCK, BLOCK), 0)
    cols = lax.broadcasted_iota(jnp.int32, (BLOCK, BLOCK), 1)
    causal = rows >= cols
    strict = rows > cols
    apart = rows ^ cols
    eye = jnp.where(rows == cols, 1.0, 0.0).astype(F32)
    heads = 2

    @pl.when(step == 0)
    def _():
        for h in range(heads):
            state[h] = jnp.concatenate([eye, jnp.zeros((DK, DV), F32)], axis=1)

    problems = []
    for b in range(blocks):
        span = slice(b * BLOCK, (b + 1) * BLOCK)
        query = proj_ref[span, 0:DK]
        key = proj_ref[span, DK : 2 * DK]
        key = key * lax.rsqrt(jnp.sum(key * key, axis=-1, keepdims=True) + 1e-06)
        qh, ql = split(query)
        kh, kl = split(key)
        stacked_h = jnp.concatenate([kh, qh], axis=0)
        stacked_l = jnp.concatenate([kl, ql], axis=0)
        products = mm(stacked_h, kh, NT) + (mm(stacked_h, kl, NT) + mm(stacked_l, kh, NT))
        key_key, query_key = products[:BLOCK], products[BLOCK:]
        for h in range(heads):
            cum_row = jnp.broadcast_to(cum_ref[h, b : b + 1, :], (BLOCK, BLOCK))
            rate_row = jnp.broadcast_to(rate_ref[h, b : b + 1, :], (BLOCK, BLOCK))
            cum_col = cum_row.T
            rate_col = rate_row.T
            ratios = jnp.where(causal, jnp.exp(jnp.where(causal, cum_col - cum_row, 0.0)), 0.0)
            weighted = ratios * rate_row
            lower = jnp.where(strict, weighted * key_key, 0.0)
            mixing = weighted * query_key
            decays = jnp.exp(cum_col)
            last = cum_col[BLOCK - 1 : BLOCK, :]
            key_tail = key * (jnp.exp(last - cum_col) * rate_col)
            value = proj_ref[span, 2 * DK + h * DV : 2 * DK + (h + 1) * DV]
            problems.append(
                dict(
                    b=b,
                    h=h,
                    lower=lower,
                    mixing=mixing,
                    right=jnp.concatenate([value, decays * key], axis=1),
                    query=decays * query,
                    key_tail=key_tail,
                    fade=jnp.exp(last) * eye,
                    inverse=eye - jnp.where(apart == 1, lower, 0.0),
                )
            )
    size = 2
    while size < BLOCK:
        for p in problems:
            part = jnp.where((apart >= size) & (apart < 2 * size), p["lower"], 0.0)
            p["inner"] = dot3_narrow(part, p["inverse"])
        for p in problems:
            p["inverse"] = p["inverse"] - dot3_narrow(p["inverse"], p["inner"])
        size *= 2
    for p in problems:
        p["solved"] = dot3_wide(p["inverse"], p["right"])
    for p in problems:
        p["mixed"] = dot3_wide(p["mixing"], p["solved"])
        p["tail"] = dot3_wide(p["key_tail"].T, p["solved"])
    for p in problems:
        h = p["h"]
        span = slice(p["b"] * BLOCK, (p["b"] + 1) * BLOCK)
        cols_h = slice(h * DV, (h + 1) * DV)
        before = state[h]
        effective = p["query"] - p["mixed"][:, DV:]
        seen = dot3_wide(effective, before)
        reach_ref[span, cols_h] = seen[:, :DK]
        base_ref[span, cols_h] = p["mixed"][:, :DV] + seen[:, DK:]
        moved = dot3_wide(p["fade"] - p["tail"][:, DV:], before)
        state[h] = jnp.concatenate([moved[:, :DK], moved[:, DK:] + p["tail"][:, :DV]], axis=1)

    @pl.when(step == pl.num_programs(0) - 1)
    def _():
        total_ref[...] = state[...].astype(total_ref.dtype)


def delta_local(proj, cumulative, rates):
    tokens = proj.shape[0]
    blocks = 8
    steps = tokens // (blocks * BLOCK)
    return pl.pallas_call(
        lambda *refs: delta_kernel(blocks, *refs),
        grid=(steps,),
        in_specs=[
            pl.BlockSpec((blocks * BLOCK, 2 * DK + 2 * DV), lambda i: (i, 0)),
            pl.BlockSpec((2, blocks, BLOCK), lambda i: (0, i, 0)),
            pl.BlockSpec((2, blocks, BLOCK), lambda i: (0, i, 0)),
        ],
        out_specs=[
            pl.BlockSpec((blocks * BLOCK, 2 * DV), lambda i: (i, 0)),
            pl.BlockSpec((blocks * BLOCK, 2 * DV), lambda i: (i, 0)),
            pl.BlockSpec((2, DK, DK + DV), lambda i: (0, 0, 0)),
        ],
        out_shape=[
            jax.ShapeDtypeStruct((tokens, 2 * DV), F32),
            jax.ShapeDtypeStruct((tokens, 2 * DV), F32),
            jax.ShapeDtypeStruct((2, DK, DK + DV), BF16),
        ],
        scratch_shapes=[pltpu.VMEM((2, DK, DK + DV), F32)],
        compiler_params=pltpu.CompilerParams(vmem_limit_bytes=40 * 2**20),
        name="delta_local",
    )(proj, cumulative, rates)


def gate_kernel(stretches, place_ref, totals_ref, base_ref, reach_ref, gate_ref, gain_ref, out_ref, entering):
    @pl.when(pl.program_id(0) == 0)
    def _():
        for h in range(2):
            entering[h] = jnp.zeros((DK, DV), F32)
        for j in range(stretches - 1):
            before = j < place_ref[0]
            for h in range(2):
                pair = totals_ref[j, h]
                high, low = split(entering[h])
                moved = mm(pair[:, :DK], jnp.concatenate([high, low], axis=1))
                moved = moved[:, :DV] + moved[:, DV:] + pair[:, DK:].astype(F32)
                entering[h] = jnp.where(before, moved, entering[h])

    for h in range(2):
        span = slice(h * DV, (h + 1) * DV)
        attended = base_ref[:, span] + dot3_narrow(reach_ref[:, span], entering[h])
        scaled = row_norm(attended, gain_ref[...], 1e-06)
        u = gate_ref[:, span]
        out_ref[:, span] = (scaled * (u / (1.0 + jnp.exp(-u)))).astype(out_ref.dtype)


def delta_gate(place, totals, base, reach, proj, gain):
    tokens = base.shape[0]
    rows = 512
    stretches = totals.shape[0]
    return pl.pallas_call(
        lambda *refs: gate_kernel(stretches, *refs),
        grid_spec=pltpu.PrefetchScalarGridSpec(
            num_scalar_prefetch=1,
            grid=(tokens // rows,),
            in_specs=[
                pl.BlockSpec((stretches, 2, DK, DK + DV), lambda i, s: (0, 0, 0, 0)),
                pl.BlockSpec((rows, 2 * DV), lambda i, s: (i, 0)),
                pl.BlockSpec((rows, 2 * DV), lambda i, s: (i, 0)),
                pl.BlockSpec((rows, 2 * DV), lambda i, s: (i, 2)),
                pl.BlockSpec((1, DV), lambda i, s: (0, 0)),
            ],
            out_specs=pl.BlockSpec((rows, 2 * DV), lambda i, s: (i, 0)),
            scratch_shapes=[pltpu.VMEM((2, DK, DV), F32)],
        ),
        out_shape=jax.ShapeDtypeStruct((tokens, 2 * DV), BF16),
        compiler_params=pltpu.CompilerParams(vmem_limit_bytes=40 * 2**20),
        name="delta_gate",
    )(place, totals, base, reach, proj, gain)


def expert_kernel(x_ref, share_ref, gate_ref, up_ref, down_ref, out_ref):
    x = x_ref[...]
    total = None
    for j in range(gate_ref.shape[0]):
        gated = mm(x, gate_ref[j])
        raised = mm(x, up_ref[j])
        hidden = gated / (1.0 + jnp.exp(-gated)) * raised * share_ref[:, j : j + 1]
        made = mm(hidden.astype(BF16), down_ref[j])
        total = made if total is None else total + made
    out_ref[...] = total.astype(out_ref.dtype)


def expert_mix(x, shares, w_gate, w_up, w_down):
    tokens, width = x.shape
    count, _, inner = w_gate.shape
    rows = 256
    whole = lambda i: (0, 0, 0)
    return pl.pallas_call(
        expert_kernel,
        grid=(tokens // rows,),
        in_specs=[
            pl.BlockSpec((rows, width), lambda i: (i, 0)),
            pl.BlockSpec((rows, count), lambda i: (i, 0)),
            pl.BlockSpec((count, width, inner), whole, pipeline_mode=pl.Buffered(1)),
            pl.BlockSpec((count, width, inner), whole, pipeline_mode=pl.Buffered(1)),
            pl.BlockSpec((count, inner, width), whole, pipeline_mode=pl.Buffered(1)),
        ],
        out_specs=pl.BlockSpec((rows, width), lambda i: (i, 0)),
        out_shape=jax.ShapeDtypeStruct((tokens, width), BF16),
        compiler_params=pltpu.CompilerParams(vmem_limit_bytes=48 * 2**20),
        name="expert_mix",
    )(x, shares, w_gate, w_up, w_down)


def local(
    tokens,
    norm_in,
    w_query,
    w_key,
    w_value,
    w_outgate,
    log_decay,
    write_rate,
    head_gain,
    w_output,
    norm_post,
    route_ids,
    route_weights,
    w_gate,
    w_up,
    w_down,
    w_shared_gate,
    w_shared_up,
    w_shared_down,
    w_shared_switch,
):
    tok_dev = tokens.shape[0]
    owners = lax.axis_size("exp")
    tok_seq = tok_dev * owners
    position = lax.axis_index("exp")
    residual_in = tokens.astype(F32)
    normed = row_norm(residual_in, norm_in, 1e-06).astype(BF16)
    w_all = jnp.concatenate([w_query, w_key, w_value, w_outgate], axis=1)
    projected = jnp.dot(
        lax.all_gather(normed, "exp", axis=0, tiled=True), w_all, preferred_element_type=F32
    )
    blocks = tok_seq // BLOCK
    cumulative = jnp.cumsum(log_decay.reshape(2, blocks, BLOCK), axis=-1)
    base, reach, total = delta_local(projected, cumulative, write_rate.reshape(2, blocks, BLOCK))
    totals = lax.all_gather(total, "seq", axis=0)
    place = lax.axis_index("seq").astype(jnp.int32).reshape(1)
    gated = delta_gate(place, totals, base, reach, projected, head_gain.reshape(1, DV))
    mixed_out = lax.psum_scatter(
        jnp.dot(gated, w_output, preferred_element_type=F32).astype(BF16),
        "exp",
        scatter_dimension=0,
        tiled=True,
    ).astype(F32)
    residual = residual_in + mixed_out
    post_norm = row_norm(residual, norm_post, 1e-06).astype(BF16)
    everyone = lax.all_gather(post_norm, "exp", axis=0, tiled=True)
    switch = jax.nn.sigmoid(jnp.dot(post_norm, w_shared_switch, preferred_element_type=F32))
    inner_act = (
        jax.nn.silu(jnp.dot(post_norm, w_shared_gate, preferred_element_type=F32))
        * jnp.dot(post_norm, w_shared_up, preferred_element_type=F32)
    ).astype(BF16)
    shared = jnp.dot(inner_act, w_shared_down, preferred_element_type=F32) * switch[:, None]
    count = w_gate.shape[0]
    mine = position * count + jnp.arange(count, dtype=jnp.int32)
    shares = jnp.sum(
        jnp.where(route_ids[:, :, None] == mine, route_weights[:, :, None], 0.0), axis=1
    )
    made = expert_mix(everyone, shares, w_gate, w_up, w_down)
    routed = lax.psum_scatter(made, "exp", scatter_dimension=0, tiled=True).astype(F32)
    return (residual + shared + routed).astype(BF16)


def solution(mesh):
    in_specs = (
        P(("seq", "exp"), None),
        P(),
        P(None, "exp"),
        P(None, "exp"),
        P(None, "exp"),
        P(None, "exp"),
        P("exp", "seq"),
        P("exp", "seq"),
        P(),
        P("exp", None),
        P(),
        P("seq", None),
        P("seq", None),
        P("exp", None, None),
        P("exp", None, None),
        P("exp", None, None),
        P(),
        P(),
        P(),
        P(),
    )
    out_specs = P(("seq", "exp"), None)
    return jax.shard_map(local, mesh=mesh, in_specs=in_specs, out_specs=out_specs, check_vma=False)
```

time: 1090 us -> 445 us (0.41)
  other arithmetic: 360 us -> 7.49 us
  matrix products: 175 us -> 21.4 us
  blocking collectives: 124 us -> 0 us
  local copies, waits for them, and re-layouts: 73.7 us -> 17.6 us
  Pallas kernels: 0 us -> 53.8 us
  waiting for transfers between devices: 311 us -> 330 us
  starting transfers between devices: 18.7 us -> 0.35 us
    another operation x8 -> x1, other arithmetic: 326 us -> 0.57 us  [local(): cumulative = jnp.cumsum(log_decay.reshape(2, blocks, BLOCK), axis=-1)]
    all_to_all x1 -> x0, waiting for transfers between devices: 148 us -> none  [local(): lax.all_to_all(produced, 'exp', split_axis=0, concat_axis=0, tiled=True)]
    dot_general x84 -> x4, matrix products: 159 us -> 11.5 us  [the longest x1 5.58 us: local(): jnp.dot(gated, w_output, preferred_element_type=F32).astype(BF16)]
    all_to_all x1 -> x0, blocking collectives: 124 us -> none  [local(): lax.all_to_all(send_rows, 'exp', split_axis=0, concat_axis=0, tiled=True)]
    reduce_scatter x1 -> x2, waiting for transfers between devices: 68.2 us -> 168 us  [the longest x1 86.8 us: local(): lax.psum_scatter(jnp.dot(gated, w_output, preferred_element_type=F32).ast...]
    all_gather x0 -> x2, waiting for transfers between devices: none -> 90.9 us  [the longest x1 69.5 us: local(): everyone = lax.all_gather(post_norm, 'exp', axis=0, tiled=True)]
    pallas_call x0 -> x3, Pallas kernels: none -> 53.8 us  [the longest x1 33.1 us: expert_mix(): pl.pallas_call(expert_kernel, grid=(tokens // rows,), in_specs=[pl.BlockS...]
    gather x2 -> x0, local copies, waits for them, and re-layouts: 26.9 us -> none  [the longest x1 16.2 us: local(): returned.reshape(experts * capacity, model_width)[targets]]
  transfers between devices with their start and end apart: 10 -> 5, of which waited for: 10 -> 5; matrix products, arithmetic and copies ran while one was open for 2% -> 1% of each run, Pallas kernels for 0% -> 0%
where the time goes in v1:
time: 445 us; the launch traced here: 444 us
  waiting for transfers between devices  330 us (74%)
  Pallas kernels  53.8 us (12%)
  matrix products  21.4 us (5%)
  local copies, waits for them, and re-layouts  17.6 us (4%)
  between operations  13.3 us (3%)
  other arithmetic  7.49 us (2%)
    reduce_scatter x1, waiting for transfers between devices, local(): lax.psum_scatter(jnp.dot(gated, w_output, preferred_element_type=F32).ast...  86.8 us
    reduce_scatter x1, waiting for transfers between devices, local(): lax.psum_scatter(made, 'exp', scatter_dimension=0, tiled=True).astype(F32)  81.5 us
    all_gather x1, waiting for transfers between devices, local(): lax.all_gather(normed, 'exp', axis=0, tiled=True)  70.7 us
    all_gather x1, waiting for transfers between devices, local(): everyone = lax.all_gather(post_norm, 'exp', axis=0, tiled=True)  69.5 us
    pallas_call x1, Pallas kernels, expert_mix(): pl.pallas_call(expert_kernel, grid=(tokens // rows,), in_specs=[pl.BlockS...  33.1 us
    all_gather x1, waiting for transfers between devices, local(): totals = lax.all_gather(total, 'seq', axis=0)  21.4 us
    pallas_call x1, Pallas kernels, delta_local(): pl.pallas_call(lambda *refs: delta_kernel(blocks, *refs), grid=(steps,),...  17.5 us
    unnamed x39, local copies, waits for them, and re-layouts  17.3 us
  transfers between devices with their start and end apart: 5, of which 5 were waited for; matrix products, arithmetic and copies ran while one was open for 1% of the time, Pallas kernels for 0%

profile of v1, /device:TPU:32, one launch (start us, length us, event | category | flops | bytes accessed | tf_op | source)
XLA Modules:
  0.0 444.0 jit_solution(11710454570532752842)
XLA Ops:
  6.5 0.0 copy-start
  6.5 0.0 all-gather.5.cloned.1.call-start
  6.5 1.4 fusion.16
  7.9 2.0 fusion.18
  10.0 0.0 all-gather.5.cloned.1.call-update
  10.0 0.0 all-gather.9.cloned.1.call-start
  10.0 0.7 copy.31
  10.8 0.7 copy.30
  11.5 0.6 reduce_window_sum.11.refs_1_
  12.0 70.7 %all-gather.5.cloned.1.call-done = bf16[2048,2048]{1,0:T(8,128)(2,1)} async-done(((bf16[128,2048]{1,0:T(8,128)(2,1)}), bf16[2048,2048]{1,0:T(8,128)(2,1)}) %all-gather.5.cloned.1.call-update) | async-done | bytes 8388624 | tf_op jit(solution)/shard_map/all_gather | solution.py:273
  82.8 9.9 %fusion.refs_0_.refs_4_ = f32[2048,768]{1,0:T(8,128)S(1)} fusion(bf16[2048,2048]{1,0:T(8,128)(2,1)} %all-gather.5.cloned.1.call-done, bf16[2048,256]{1,0:T(8,128)(2,1)} %param.25, bf16[2048,256]{1,0:T(8,128)(2,1)} %param.24, bf16[2048,128]{1,0:T(8,128)(2,1)} %param.23, bf16[2048,128]{1,0:T(8,128)(2,1)} %param.22), kind=kOutput, calls=%fused_computation.1 | convolution fusion | flops 6455033856 | bytes 17825792 | tf_op jit(solution)/shard_map/dot_general | solution.py:272
  92.7 0.0 copy-start.9
  92.7 17.5 %delta_local.1 = (f32[2048,256]{1,0:T(8,128)S(1)}, f32[2048,256]{1,0:T(8,128)S(1)}, bf16[2,128,256]{2,1,0:T(8,128)(2,1)}) custom-call(f32[2048,768]{1,0:T(8,128)S(1)} %fusion.refs_0_.refs_4_, f32[2,16,128]{2,1,0:T(8,128)S(1)} %reduce_window_sum.11.refs_1_, f32[2,16,128]{2,1,0:T(8,128)S(1)} %bitcast.32), custom_call_target="tpu_custom_call" | custom-call | tf_op jit(solution)/shard_map/delta_local/pallas_call | solution.py:138
  110.2 2.7 copy-done.1
  112.8 1.4 copy-done.4
  114.2 1.4 copy-done.6
  115.6 0.0 all-gather.9.cloned.1.call-update
  115.6 0.2 reduce-scatter.3.cloned.1.call-start
  115.8 21.4 %all-gather.9.cloned.1.call-done = bf16[16,128,256]{2,1,0:T(8,128)(2,1)} async-done(((bf16[2,128,256]{2,1,0:T(8,128)(2,1)}), bf16[16,128,256]{2,1,0:T(8,128)(2,1)}) %all-gather.9.cloned.1.call-update) | async-done | bytes 1048592 | tf_op jit(solution)/shard_map/all_gather | solution.py:278
  137.2 0.0 copy-done.9
  137.2 2.8 copy-done.2
  140.0 1.6 copy-done.5
  141.6 1.6 copy-done.7
  143.2 1.2 copy-done.8
  144.4 3.2 delta_gate.1
  147.7 0.0 copy-done.13
  147.7 5.6 %convolution_convert_fusion = bf16[2048,2048]{1,0:T(8,128)(2,1)} fusion(bf16[2048,256]{1,0:T(8,128)(2,1)S(1)} %delta_gate.1, bf16[256,2048]{1,0:T(8,128)(2,1)S(1)} %copy-done.13), kind=kOutput, calls=%fused_computation | convolution fusion | flops 2151677952 | bytes 10485760 | tf_op jit(solution)/shard_map/dot_general | solution.py:282
  153.3 0.0 reduce-scatter.3.cloned.1.call-update
  153.3 0.0 all-gather.7.cloned.1.call-start
  153.4 86.8 %reduce-scatter.3.cloned.1.call-done = bf16[128,2048]{1,0:T(8,128)(2,1)} async-done(((bf16[2048,2048]{1,0:T(8,128)(2,1)}), bf16[128,2048]{1,0:T(8,128)(2,1)}) %reduce-scatter.3.cloned.1.call-update) | async-done | bytes 524304 | tf_op jit(solution)/shard_map/reduce_scatter | solution.py:281
  240.1 0.0 copy-done.10
  240.1 1.3 multiply_reduce_fusion
  241.4 0.0 copy-done.16
  241.5 2.0 multiply_convert_fusion
  243.5 0.0 all-gather.7.cloned.1.call-update
  243.5 0.0 reduce-scatter.5.cloned.1.call-start
  243.6 0.2 fusion.24
  243.8 0.4 copy.25.share_ref
  244.1 69.5 %all-gather.7.cloned.1.call-done.x_ref = bf16[2048,2048]{1,0:T(8,128)(2,1)} async-done(((bf16[128,2048]{1,0:T(8,128)(2,1)}), bf16[2048,2048]{1,0:T(8,128)(2,1)}) %all-gather.7.cloned.1.call-update) | async-done | bytes 8388624 | tf_op jit(solution)/shard_map/all_gather | solution.py:289
  313.7 2.2 copy-done.3
  315.9 33.1 %expert_mix.1 = bf16[2048,2048]{1,0:T(8,128)(2,1)} custom-call(bf16[2048,2048]{1,0:T(8,128)(2,1)} %all-gather.7.cloned.1.call-done.x_ref, f32[2048,2]{1,0:T(8,128)S(1)} %copy.25.share_ref, bf16[2,2048,512]{2,1,0:T(8,128)(2,1)S(1)} %copy-done.3, bf16[2,2048,512]{2,1,0:T(8,128)(2,1)} %up_ref.1, bf16[2,512,2048]{2,1,0:T(8,128)(2,1)} %down_ref.1), custom_call_target="tpu_custom_call" | custom-call | tf_op jit(solution)/shard_map/expert_mix/pallas_call | solution.py:226
  349.0 0.0 reduce-scatter.5.cloned.1.call-update
  349.0 0.7 copy-done.17
  349.7 0.4 copy-done.12
  350.0 0.2 fusion.15
  350.3 2.1 fusion.28
  352.3 81.5 %reduce-scatter.5.cloned.1.call-done = bf16[128,2048]{1,0:T(8,128)(2,1)} async-done(((bf16[2048,2048]{1,0:T(8,128)(2,1)}), bf16[128,2048]{1,0:T(8,128)(2,1)}) %reduce-scatter.5.cloned.1.call-update) | async-done | bytes 524304 | tf_op jit(solution)/shard_map/reduce_scatter | solution.py:302
  433.9 3.6 fusion.10
  (24 shorter events, 0.1 us)
Async XLA Ops:
  6.5 427.3 %copy-start = (bf16[512,2048]{1,0:T(8,128)(2,1)S(1)}, bf16[512,2048]{1,0:T(8,128)(2,1)}, u32[]{:S(2)}) copy-start(bf16[512,2048]{1,0:T(8,128)(2,1)} %param.38) | copy-start | bytes 6291460
  6.5 76.2 %all-gather.5.cloned.1.call-start = ((), (), s32[]{:S(2)}) async-start(), calls=%async_computation.2 | async-start | bytes 8912896 | tf_op jit(solution)/shard_map/all_gather | solution.py:273
  10.0 127.2 %all-gather.9.cloned.1.call-start = ((), (), s32[]{:S(2)}) async-start(), calls=%async_computation.6 | async-start | bytes 1179648 | tf_op jit(solution)/shard_map/all_gather | solution.py:278
  92.7 44.5 %copy-start.9 = (f32[128]{0:T(128)S(1)}, f32[128]{0:T(128)}, u32[]{:S(2)}) copy-start(f32[128]{0:T(128)} %param.28) | copy-start | bytes 1540
  110.2 2.7 copy-start.1
  112.8 1.4 copy-start.4
  114.2 1.4 copy-start.6
  115.6 124.5 %reduce-scatter.3.cloned.1.call-start = ((), (), s32[]{:S(2)}) async-start(), calls=%async_computation.3 | async-start | bytes 8912896 | tf_op jit(solution)/shard_map/reduce_scatter | solution.py:281
  137.2 2.8 copy-start.2
  140.0 1.6 copy-start.5
  141.6 1.6 copy-start.7
  143.2 1.2 copy-start.8
  144.4 3.3 copy-start.13
  153.3 86.9 %copy-start.10 = (bf16[128,2048]{1,0:T(8,128)(2,1)S(1)}, bf16[128,2048]{1,0:T(8,128)(2,1)}, u32[]{:S(2)}) copy-start(bf16[128,2048]{1,0:T(8,128)(2,1)} %param.20) | copy-start | bytes 1572868
  153.3 88.2 %copy-start.16 = (f32[2048]{0:T(1024)S(1)}, f32[2048]{0:T(1024)}, u32[]{:S(2)}) copy-start(f32[2048]{0:T(1024)} %param.30) | copy-start | bytes 24580
  153.3 90.3 %copy-start.14 = (f32[2048,10]{0,1:T(8,128)S(1)}, f32[2048,10]{0,1:T(8,128)}, u32[]{:S(2)}) copy-start(f32[2048,10]{0,1:T(8,128)} %param.32) | copy-start | bytes 245764
  153.3 90.3 %copy-start.15 = (s32[2048,10]{0,1:T(8,128)S(1)}, s32[2048,10]{0,1:T(8,128)}, u32[]{:S(2)}) copy-start(s32[2048,10]{0,1:T(8,128)} %param.31) | copy-start | bytes 245764
  153.3 160.4 %all-gather.7.cloned.1.call-start = ((), (), s32[]{:S(2)}) async-start(), calls=%async_computation.4 | async-start | bytes 8912896 | tf_op jit(solution)/shard_map/all_gather | solution.py:289
  243.5 190.4 %reduce-scatter.5.cloned.1.call-start = ((), (), s32[]{:S(2)}) async-start(), calls=%async_computation.5 | async-start | bytes 8912896 | tf_op jit(solution)/shard_map/reduce_scatter | solution.py:302
  313.7 2.2 copy-start.3
  349.0 0.7 copy-start.17
  349.0 1.1 copy-start.12
  349.0 84.9 %copy-start.11 = (bf16[128,2048]{1,0:T(8,128)(2,1)S(1)}, bf16[128,2048]{1,0:T(8,128)(2,1)}, u32[]{:S(2)}) copy-start(bf16[128,2048]{1,0:T(8,128)(2,1)} %param.20) | copy-start | bytes 1572868
Sparse Core Ops, SparseCore 0:
  10.1 72.6 all-gather.4
  115.7 21.4 all-gather.8
  153.4 86.6 reduce-scatter.2
  243.6 70.0 all-gather.6
  349.1 84.7 reduce-scatter.4
